TPU v7x, 32 devices: a whole 2x2x4 slice. The times are simulated.
32 devices in a mesh: gx: 8 (over y, x, core), gy: 4 (over z).
Axes of the slice: x: 2, y: 2, z: 4, core: 2. Of those that a mesh axis runs over, the one named last changes fastest.
Arguments:
- u_flow: bfloat16 [16, 1152, 512], P(None, 'gx', 'gy'), may hold values from -6 to 6
- v_flow: bfloat16 [16, 1152, 512], P(None, 'gx', 'gy'), may hold values from -6 to 6
- sea_mask: int32 [1152, 512], P('gx', 'gy'), may hold values 0 or 1
- bottom_level: int32 [1152, 512], P('gx', 'gy'), may hold values from 1 to 16
- mode_project: bfloat16 [16, 2], replicated, may hold values from -1.5 to 1.5
- mode_shape: float32 [16, 2], replicated, may hold values from -4 to 4
- forward_x: bfloat16 [1152, 1152], P('gx'), may hold values from -0.1875 to 0.1875
- forward_y: bfloat16 [512, 512], P('gy'), may hold values from -0.25 to 0.25
- inverse_x: bfloat16 [1152, 1152], P('gx'), may hold values from -0.1875 to 0.1875
- inverse_y: bfloat16 [512, 512], P('gy'), may hold values from -0.25 to 0.25
- eigen_x: float32 [1152], P('gx'), may hold values from 0.5 to 4
- eigen_y: float32 [512], P('gy'), may hold values from 0.5 to 4
- mode_shift: float32 [2], replicated, may hold values from 0.5 to 2
Outputs:
- u_correct: bfloat16 [16, 1152, 512], P(None, 'gx', 'gy')
- v_correct: bfloat16 [16, 1152, 512], P(None, 'gx', 'gy')
- pressure: float32 [2, 1152, 512], P(None, 'gx', 'gy')
Inputs may be any that keep to these rules, and one draw needn't show every extreme that they name: `sea_mask`: land and sea flags.
All inputs are finite; a program needn't handle non-finite values. No bound on the sum of `sea_mask` on one device may be relied on, other than what follows from the above.
Results may differ from a plain program's by a relative error of at most 0.014.
Values may be sent and summed in bfloat16 or wider, within the bound.
A program may use at most 64 MiB of HBM per device.

v0:
```python
import jax
import jax.numpy as jnp
from jax import lax
from jax.sharding import PartitionSpec as P


def extended(block, sides, width, periodic):
    for axis, dim in sides:
        count = lax.axis_size(axis)
        forward = [(i, i + 1) for i in range(count - 1)]
        if periodic:
            forward.append((count - 1, 0))
        backward = [(target, source) for source, target in forward]
        low = lax.ppermute(
            lax.slice_in_dim(block, block.shape[dim] - width, None, axis=dim), axis, forward
        )
        high = lax.ppermute(lax.slice_in_dim(block, 0, width, axis=dim), axis, backward)
        block = jnp.concatenate([low, block, high], axis=dim)
    return block


def centre_x(field):
    padded = extended(field.astype(jnp.bfloat16), (("gx", 1),), 1, True).astype(field.dtype)
    return 0.5 * (padded[:, 2:, :] - padded[:, :-2, :])


def centre_y(field):
    padded = extended(field.astype(jnp.bfloat16), (("gy", 2),), 1, False).astype(field.dtype)
    return 0.5 * (padded[:, :, 2:] - padded[:, :, :-2])


def fold_x(data, table):
    return jnp.einsum(
        "kn,mnj->mkj",
        table,
        lax.all_gather(data, "gx", axis=1, tiled=True),
        preferred_element_type=jnp.float32,
    )


def transform_x(data, table):
    return jnp.concatenate(
        [fold_x(data[mode : mode + 1], table) for mode in range(data.shape[0])], 0
    )


def transform_y(data, table):
    return jnp.einsum(
        "min,kn->mik",
        lax.all_gather(data, "gy", axis=2, tiled=True),
        table,
        preferred_element_type=jnp.float32,
    )


def body(
    u_flow,
    v_flow,
    sea_mask,
    bottom_level,
    mode_project,
    mode_shape,
    forward_x,
    forward_y,
    inverse_x,
    inverse_y,
    eigen_x,
    eigen_y,
    mode_shift,
):
    level_ids = lax.broadcasted_iota(jnp.int32, u_flow.shape, 0)
    wet_int = sea_mask[None] * (level_ids < bottom_level[None]).astype(jnp.int32)
    wet = wet_int.astype(jnp.bfloat16)
    flux_u = jnp.einsum(
        "lm,lij->mij", mode_project, u_flow * wet, preferred_element_type=jnp.float32
    )
    flux_v = jnp.einsum(
        "lm,lij->mij", mode_project, v_flow * wet, preferred_element_type=jnp.float32
    )
    flux_u = flux_u.astype(jnp.bfloat16).astype(jnp.float32)
    flux_v = flux_v.astype(jnp.bfloat16).astype(jnp.float32)
    mask_f = sea_mask.astype(jnp.float32)
    divergence = (mask_f[None] * (centre_x(flux_u) + centre_y(flux_v))).astype(jnp.bfloat16)
    spec_x = transform_x(divergence, forward_x).astype(jnp.bfloat16)
    spec_xy = transform_y(spec_x, forward_y)
    denom = eigen_x[None, :, None] + eigen_y[None, None, :] + mode_shift[:, None, None]
    scaled = (spec_xy / denom).astype(jnp.bfloat16)
    back_y = transform_y(scaled, inverse_y).astype(jnp.bfloat16)
    pressure = transform_x(back_y, inverse_x)
    grad_x = centre_x(pressure)
    grad_y = centre_y(pressure)
    wet_f = wet_int.astype(jnp.float32)
    shape_zero = mode_shape[:, 0][:, None, None]
    shape_one = mode_shape[:, 1][:, None, None]
    u_correct = (-wet_f * (shape_zero * grad_x[0][None] + shape_one * grad_x[1][None])).astype(
        jnp.bfloat16
    )
    v_correct = (-wet_f * (shape_zero * grad_y[0][None] + shape_one * grad_y[1][None])).astype(
        jnp.bfloat16
    )
    return (u_correct, v_correct, pressure)


def solution(mesh):
    return jax.shard_map(
        body,
        mesh=mesh,
        in_specs=(
            P(None, "gx", "gy"),
            P(None, "gx", "gy"),
            P("gx", "gy"),
            P("gx", "gy"),
            P(),
            P(),
            P("gx", None),
            P("gy", None),
            P("gx", None),
            P("gy", None),
            P("gx"),
            P("gy"),
            P(),
        ),
        out_specs=(P(None, "gx", "gy"), P(None, "gx", "gy"), P(None, "gx", "gy")),
        check_vma=False,
    )
```

profile of v0, /device:TPU:0, one launch (start us, length us, event | category | flops | bytes accessed | tf_op | source)
XLA Modules:
  0.0 95.5 jit_solution(6575015127694259134)
XLA Ops:
  0.6 0.0 copy-start
  0.7 1.7 %fusion.11 = (bf16[16,144,128]{2,1,0:T(8,128)(2,1)S(1)}, bf16[16,144,128]{2,1,0:T(8,128)(2,1)S(1)}) fusion(bf16[16,144,128]{2,1,0:T(8,128)(2,1)} %param.13, s32[144,128]{1,0:T(8,128)} %param.15, s32[144,128]{1,0:T(8,128)} %param.16, bf16[16,144,128]{2,1,0:T(8,128)(2,1)} %param.14), kind=kLoop, calls=%fused_computation.22 | loop fusion | flops 2949120 | bytes 2506752 | tf_op jit(solution)/shard_map/mul | solution.py:75
  2.3 0.2 fusion.6
  2.6 0.0 copy-start.2
  2.6 0.5 collective-permute-start
  3.1 2.9 %collective-permute-start.1 = (bf16[2,1,128]{2,0,1:T(2,128)(2,1)S(1)}, bf16[2,1,128]{2,0,1:T(2,128)(2,1)S(1)}, u32[]{:S(2)}, u32[]{:S(2)}) collective-permute-start(bf16[2,1,128]{2,0,1:T(2,128)(2,1)S(1)} %get-tuple-element.22), channel_id=1, source_target_pairs={{4,0},{8,4},{12,8},{16,12},{20,16},{24,20},{28,24},{0,28},{5,1},{9... | collective-permute-start | bytes 1544 | tf_op jit(solution)/shard_map/ppermute | solution.py:17
  6.0 0.2 fusion.7
  6.3 0.1 fusion.33
  6.4 4.2 %collective-permute-start.2 = (bf16[2,144,1]{2,0,1:T(2,128)(2,1)S(1)}, bf16[2,144,1]{2,0,1:T(2,128)(2,1)S(1)}, u32[]{:S(2)}, u32[]{:S(2)}) collective-permute-start(bf16[2,144,1]{2,0,1:T(2,128)(2,1)S(1)} %get-tuple-element.23), channel_id=1, source_target_pairs={{0,1},{1,2},{2,3},{4,5},{5,6},{6,7},{8,9},{9,10},{10,11},{12,13},{... | collective-permute-start | bytes 1736 | tf_op jit(solution)/shard_map/ppermute | solution.py:14
  10.6 1.3 %collective-permute-start.3 = (bf16[2,144,1]{2,0,1:T(2,128)(2,1)S(1)}, bf16[2,144,1]{2,0,1:T(2,128)(2,1)S(1)}, u32[]{:S(2)}, u32[]{:S(2)}) collective-permute-start(bf16[2,144,1]{2,0,1:T(2,128)(2,1)S(1)} %get-tuple-element.24), channel_id=1, source_target_pairs={{1,0},{2,1},{3,2},{5,4},{6,5},{7,6},{9,8},{10,9},{11,10},{13,12},{... | collective-permute-start | bytes 1736 | tf_op jit(solution)/shard_map/ppermute | solution.py:17
  11.9 0.1 broadcast_add_fusion
  12.1 0.0 collective-permute-done
  12.1 0.0 collective-permute-done.1
  12.1 0.1 maximum_convert_fusion.3
  12.2 0.4 collective-permute-done.2
  12.6 4.3 %collective-permute-done.3 = bf16[2,144,1]{2,0,1:T(2,128)(2,1)S(1)} collective-permute-done((bf16[2,144,1]{2,0,1:T(2,128)(2,1)S(1)}, bf16[2,144,1]{2,0,1:T(2,128)(2,1)S(1)}, u32[]{:S(2)}, u32[]{:S(2)}) %collective-permute-start.3) | collective-permute-done | bytes 608 | tf_op jit(solution)/shard_map/ppermute | solution.py:17
  16.8 0.4 maximum_convert_fusion
  17.2 0.2 fusion.22
  17.5 0.1 fusion.31
  17.6 9.5 %all_gather.19 = bf16[1,1152,128]{2,1,0:T(8,128)(2,1)S(1)} all-gather(bf16[1,144,128]{2,1,0:T(8,128)(2,1)S(1)} %copy.23), channel_id=1, replica_groups=mesh['gx'=8,'gy'=4] {'gx'}, dimensions={1}, use_global_device_ids=true | all-gather | bytes 331776 | tf_op jit(solution)/shard_map/all_gather | solution.py:36
  27.1 8.5 %all_gather.18 = bf16[1,1152,128]{2,1,0:T(8,128)(2,1)S(1)} all-gather(bf16[1,144,128]{2,1,0:T(8,128)(2,1)S(1)} %copy.22), channel_id=1, replica_groups=mesh['gx'=8,'gy'=4] {'gx'}, dimensions={1}, use_global_device_ids=true | all-gather | bytes 331776 | tf_op jit(solution)/shard_map/all_gather | solution.py:36
  35.6 0.3 fusion.9
  35.9 0.0 copy-start.8
  35.9 0.0 copy-start.10
  35.9 0.3 fusion.8
  36.2 13.9 %all_gather.20 = bf16[2,144,512]{2,1,0:T(8,128)(2,1)S(1)} all-gather(bf16[2,144,128]{2,1,0:T(8,128)(2,1)S(1)} %pad_maximum_fusion.1), channel_id=1, replica_groups=mesh['gx'=8,'gy'=4] {'gy'}, dimensions={2}, use_global_device_ids=true | all-gather | bytes 368640 | tf_op jit(solution)/shard_map/all_gather | solution.py:50
  50.1 0.2 fusion.5
  50.3 12.9 %all_gather.21 = bf16[2,144,512]{2,1,0:T(8,128)(2,1)S(1)} all-gather(bf16[2,144,128]{2,1,0:T(8,128)(2,1)S(1)} %fusion.5), channel_id=1, replica_groups=mesh['gx'=8,'gy'=4] {'gy'}, dimensions={2}, use_global_device_ids=true | all-gather | bytes 368640 | tf_op jit(solution)/shard_map/all_gather | solution.py:50
  63.3 0.2 convolution_convert_fusion.2
  63.5 9.4 %all_gather.22 = bf16[1,1152,128]{2,1,0:T(8,128)(2,1)S(1)} all-gather(bf16[1,144,128]{2,1,0:T(8,128)(2,1)S(1)} %get-tuple-element.17), channel_id=1, replica_groups=mesh['gx'=8,'gy'=4] {'gx'}, dimensions={1}, use_global_device_ids=true | all-gather | bytes 331776 | tf_op jit(solution)/shard_map/all_gather | solution.py:36
  72.9 8.5 %all_gather.23 = bf16[1,1152,128]{2,1,0:T(8,128)(2,1)S(1)} all-gather(bf16[1,144,128]{2,1,0:T(8,128)(2,1)S(1)} %get-tuple-element.18), channel_id=1, replica_groups=mesh['gx'=8,'gy'=4] {'gx'}, dimensions={1}, use_global_device_ids=true | all-gather | bytes 331776 | tf_op jit(solution)/shard_map/all_gather | solution.py:36
  81.4 0.3 convolution_bitcast_fusion.1
  81.7 0.3 convolution_bitcast_fusion
  81.9 0.7 fusion.27
  82.6 0.4 collective-permute-start.4
  83.0 2.3 %collective-permute-start.5 = (bf16[2,1,128]{2,1,0:T(2,128)(2,1)S(1)}, bf16[2,1,128]{2,1,0:T(2,128)(2,1)S(1)}, u32[]{:S(2)}, u32[]{:S(2)}) collective-permute-start(bf16[2,1,128]{2,1,0:T(2,128)(2,1)S(1)} %get-tuple-element.16), channel_id=1, source_target_pairs={{4,0},{8,4},{12,8},{16,12},{20,16},{24,20},{28,24},{0,28},{5,1},{9... | collective-permute-start | bytes 1544 | tf_op jit(solution)/shard_map/ppermute | solution.py:17
  85.3 0.1 fusion.28
  85.4 1.3 %collective-permute-start.6 = (bf16[2,144,1]{2,1,0:T(8,128)(2,1)S(1)}, bf16[2,144,1]{2,1,0:T(8,128)(2,1)S(1)}, u32[]{:S(2)}, u32[]{:S(2)}) collective-permute-start(bf16[2,144,1]{2,1,0:T(8,128)(2,1)S(1)} %get-tuple-element.13), channel_id=1, source_target_pairs={{0,1},{1,2},{2,3},{4,5},{5,6},{6,7},{8,9},{9,10},{10,11},{12,13},{... | collective-permute-start | bytes 1736 | tf_op jit(solution)/shard_map/ppermute | solution.py:14
  86.7 1.3 %collective-permute-start.7 = (bf16[2,144,1]{2,1,0:T(8,128)(2,1)S(1)}, bf16[2,144,1]{2,1,0:T(8,128)(2,1)S(1)}, u32[]{:S(2)}, u32[]{:S(2)}) collective-permute-start(bf16[2,144,1]{2,1,0:T(8,128)(2,1)S(1)} %get-tuple-element.14), channel_id=1, source_target_pairs={{1,0},{2,1},{3,2},{5,4},{6,5},{7,6},{9,8},{10,9},{11,10},{13,12},{... | collective-permute-start | bytes 1736 | tf_op jit(solution)/shard_map/ppermute | solution.py:17
  88.0 0.0 collective-permute-done.4
  88.0 0.0 collective-permute-done.5
  88.0 0.6 collective-permute-done.6
  88.6 4.3 %collective-permute-done.7 = bf16[2,144,1]{2,1,0:T(8,128)(2,1)S(1)} collective-permute-done((bf16[2,144,1]{2,1,0:T(8,128)(2,1)S(1)}, bf16[2,144,1]{2,1,0:T(8,128)(2,1)S(1)}, u32[]{:S(2)}, u32[]{:S(2)}) %collective-permute-start.7) | collective-permute-done | bytes 608 | tf_op jit(solution)/shard_map/ppermute | solution.py:17
  92.9 0.1 maximum_convert_fusion.1
  93.1 0.0 copy-start.3
  93.1 0.1 fusion.18
  93.2 0.7 copy-done.3
  94.0 1.6 %fusion.4 = (bf16[16,144,128]{2,1,0:T(8,128)(2,1)}, bf16[16,144,128]{2,1,0:T(8,128)(2,1)}) fusion(f32[144,128]{1,0:T(8,128)S(1)} %get-tuple-element.8, f32[144,128]{1,0:T(8,128)S(1)} %get-tuple-element.7, f32[16]{0:T(128)S(1)} %get-tuple-element.26, f32[16]{0:T(128)S(1)} %get-tuple-element.25, s32[144,128]{1,0:T(8,128)S(1)} %copy-done.2, ...), kind=kLoop, calls=%fused_computation.6 | loop fusion | flops 4128768 | bytes 1622144 | tf_op jit(solution)/shard_map/convert_element_type | solution.py:98
  (27 shorter events, 0.2 us)
Async XLA Ops:
  0.6 35.0 %copy-start = (bf16[144,1152]{1,0:T(8,128)(2,1)S(1)}, bf16[144,1152]{1,0:T(8,128)(2,1)}, u32[]{:S(2)}) copy-start(bf16[144,1152]{1,0:T(8,128)(2,1)} %param.19) | copy-start | bytes 995332
  0.6 1.7 %copy-start.9 = (bf16[16,2]{0,1:T(2,128)(2,1)S(1)}, bf16[16,2]{0,1:T(2,128)(2,1)}, u32[]{:S(2)}) copy-start(bf16[16,2]{0,1:T(2,128)(2,1)} %param.17) | copy-start | bytes 196
  2.6 9.3 %copy-start.2 = (s32[144,128]{1,0:T(8,128)S(1)}, s32[144,128]{1,0:T(8,128)}, u32[]{:S(2)}) copy-start(s32[144,128]{1,0:T(8,128)} %param.15) | copy-start | bytes 221188
  2.6 9.5 %collective-permute-start = (bf16[2,1,128]{2,0,1:T(2,128)(2,1)S(1)}, bf16[2,1,128]{2,0,1:T(2,128)(2,1)S(1)}, u32[]{:S(2)}, u32[]{:S(2)}) collective-permute-start(bf16[2,1,128]{2,0,1:T(2,128)(2,1)S(1)} %get-tuple-element.21), channel_id=1, source_target_pairs={{0,4},{4,8},{8,12},{12,16},{16,20},{20,24},{24,28},{28,0},{1,5},{5... | collective-permute-start | bytes 1544 | tf_op jit(solution)/shard_map/ppermute | solution.py:14
  3.1 9.0 %collective-permute-start.1 = (bf16[2,1,128]{2,0,1:T(2,128)(2,1)S(1)}, bf16[2,1,128]{2,0,1:T(2,128)(2,1)S(1)}, u32[]{:S(2)}, u32[]{:S(2)}) collective-permute-start(bf16[2,1,128]{2,0,1:T(2,128)(2,1)S(1)} %get-tuple-element.22), channel_id=1, source_target_pairs={{4,0},{8,4},{12,8},{16,12},{20,16},{24,20},{28,24},{0,28},{5,1},{9... | collective-permute-start | bytes 1544 | tf_op jit(solution)/shard_map/ppermute | solution.py:17
  6.0 5.9 %copy-start.5 = (f32[144]{0:T(256)S(1)}, f32[144]{0:T(256)}, u32[]{:S(2)}) copy-start(f32[144]{0:T(256)} %param.23) | copy-start | bytes 1732
  6.0 5.9 %copy-start.7 = (f32[128]{0:T(128)S(1)}, f32[128]{0:T(128)}, u32[]{:S(2)}) copy-start(f32[128]{0:T(128)} %param.24) | copy-start | bytes 1540
  6.0 6.0 %copy-start.6 = (f32[16,2]{0,1:T(2,128)S(1)}, f32[16,2]{0,1:T(2,128)}, u32[]{:S(2)}) copy-start(f32[16,2]{0,1:T(2,128)} %param.18) | copy-start | bytes 388
  6.4 6.1 %collective-permute-start.2 = (bf16[2,144,1]{2,0,1:T(2,128)(2,1)S(1)}, bf16[2,144,1]{2,0,1:T(2,128)(2,1)S(1)}, u32[]{:S(2)}, u32[]{:S(2)}) collective-permute-start(bf16[2,144,1]{2,0,1:T(2,128)(2,1)S(1)} %get-tuple-element.23), channel_id=1, source_target_pairs={{0,1},{1,2},{2,3},{4,5},{5,6},{6,7},{8,9},{9,10},{10,11},{12,13},{... | collective-permute-start | bytes 1736 | tf_op jit(solution)/shard_map/ppermute | solution.py:14
  10.6 6.2 %collective-permute-start.3 = (bf16[2,144,1]{2,0,1:T(2,128)(2,1)S(1)}, bf16[2,144,1]{2,0,1:T(2,128)(2,1)S(1)}, u32[]{:S(2)}, u32[]{:S(2)}) collective-permute-start(bf16[2,144,1]{2,0,1:T(2,128)(2,1)S(1)} %get-tuple-element.24), channel_id=1, source_target_pairs={{1,0},{2,1},{3,2},{5,4},{6,5},{7,6},{9,8},{10,9},{11,10},{13,12},{... | collective-permute-start | bytes 1736 | tf_op jit(solution)/shard_map/ppermute | solution.py:17
  35.9 14.2 %copy-start.8 = (bf16[128,512]{1,0:T(8,128)(2,1)S(1)}, bf16[128,512]{1,0:T(8,128)(2,1)}, u32[]{:S(2)}) copy-start(bf16[128,512]{1,0:T(8,128)(2,1)} %param.20) | copy-start | bytes 393220
  35.9 14.2 %copy-start.10 = (f32[2]{0:T(128)S(1)}, f32[2]{0:T(128)}, u32[]{:S(2)}) copy-start(f32[2]{0:T(128)} %param.25) | copy-start | bytes 28
  50.1 13.2 %copy-start.4 = (bf16[128,512]{1,0:T(8,128)(2,1)S(1)}, bf16[128,512]{1,0:T(8,128)(2,1)}, u32[]{:S(2)}) copy-start(bf16[128,512]{1,0:T(8,128)(2,1)} %param.22) | copy-start | bytes 393220
  63.2 18.1 %copy-start.1 = (bf16[144,1152]{1,0:T(8,128)(2,1)S(1)}, bf16[144,1152]{1,0:T(8,128)(2,1)}, u32[]{:S(2)}) copy-start(bf16[144,1152]{1,0:T(8,128)(2,1)} %param.21) | copy-start | bytes 995332
  82.6 5.3 %collective-permute-start.4 = (bf16[2,1,128]{2,1,0:T(2,128)(2,1)S(1)}, bf16[2,1,128]{2,1,0:T(2,128)(2,1)S(1)}, u32[]{:S(2)}, u32[]{:S(2)}) collective-permute-start(bf16[2,1,128]{2,1,0:T(2,128)(2,1)S(1)} %get-tuple-element.15), channel_id=1, source_target_pairs={{0,4},{4,8},{8,12},{12,16},{16,20},{20,24},{24,28},{28,0},{1,5},{5... | collective-permute-start | bytes 1544 | tf_op jit(solution)/shard_map/ppermute | solution.py:14
  83.0 5.0 %collective-permute-start.5 = (bf16[2,1,128]{2,1,0:T(2,128)(2,1)S(1)}, bf16[2,1,128]{2,1,0:T(2,128)(2,1)S(1)}, u32[]{:S(2)}, u32[]{:S(2)}) collective-permute-start(bf16[2,1,128]{2,1,0:T(2,128)(2,1)S(1)} %get-tuple-element.16), channel_id=1, source_target_pairs={{4,0},{8,4},{12,8},{16,12},{20,16},{24,20},{28,24},{0,28},{5,1},{9... | collective-permute-start | bytes 1544 | tf_op jit(solution)/shard_map/ppermute | solution.py:17
  85.4 3.3 %collective-permute-start.6 = (bf16[2,144,1]{2,1,0:T(8,128)(2,1)S(1)}, bf16[2,144,1]{2,1,0:T(8,128)(2,1)S(1)}, u32[]{:S(2)}, u32[]{:S(2)}) collective-permute-start(bf16[2,144,1]{2,1,0:T(8,128)(2,1)S(1)} %get-tuple-element.13), channel_id=1, source_target_pairs={{0,1},{1,2},{2,3},{4,5},{5,6},{6,7},{8,9},{9,10},{10,11},{12,13},{... | collective-permute-start | bytes 1736 | tf_op jit(solution)/shard_map/ppermute | solution.py:14
  86.7 6.3 %collective-permute-start.7 = (bf16[2,144,1]{2,1,0:T(8,128)(2,1)S(1)}, bf16[2,144,1]{2,1,0:T(8,128)(2,1)S(1)}, u32[]{:S(2)}, u32[]{:S(2)}) collective-permute-start(bf16[2,144,1]{2,1,0:T(8,128)(2,1)S(1)} %get-tuple-element.14), channel_id=1, source_target_pairs={{1,0},{2,1},{3,2},{5,4},{6,5},{7,6},{9,8},{10,9},{11,10},{13,12},{... | collective-permute-start | bytes 1736 | tf_op jit(solution)/shard_map/ppermute | solution.py:17
  93.1 0.9 copy-start.3
where the time goes:
time: 95.9 us; the launch traced here: 95.5 us
  blocking collectives  62.7 us (65%)
  starting transfers between devices  14.1 us (15%)
  waiting for transfers between devices  9.56 us (10%)
  other arithmetic  5.01 us (5%)
  matrix products  1.96 us (2%)
  local copies, waits for them, and re-layouts  1.19 us (1%)
  between operations  0.98 us (1%)
    all_gather x4, blocking collectives, fold_x(): lax.all_gather(data, 'gx', axis=1, tiled=True)  35.8 us
    all_gather x2, blocking collectives, transform_y(): lax.all_gather(data, 'gy', axis=2, tiled=True)  26.8 us
    ppermute x4, waiting for transfers between devices, extended(): lax.ppermute(lax.slice_in_dim(block, 0, width, axis=dim), axis, backward)  8.61 us
    ppermute x4, starting transfers between devices, extended(): lax.ppermute(lax.slice_in_dim(block, 0, width, axis=dim), axis, backward)  7.83 us
    ppermute x4, starting transfers between devices, extended(): lax.ppermute(lax.slice_in_dim(block, block.shape[dim] - width, None, axis...  6.32 us
  transfers between devices with their start and end apart: 8, of which 4 were waited for; matrix products, arithmetic and copies ran while one was open for 1% of the time, Pallas kernels for 0%

commit v1 on v0

v1 whole, which is shorter than its diff:
```python
import functools

import jax
import jax.numpy as jnp
from jax import lax
from jax.experimental import pallas as pl
from jax.experimental.pallas import tpu as pltpu
from jax.sharding import PartitionSpec as P

F32, BF16 = jnp.float32, jnp.bfloat16
ROWS = 16
PAD = 8
MESH = pl.DeviceIdType.MESH
LAST = (((1,), (1,)), ((), ()))


def remote(src, dst, send, recv, **device):
    return pltpu.make_async_remote_copy(
        src_ref=src, dst_ref=dst, send_sem=send, recv_sem=recv, device_id=device, device_id_type=MESH
    )


def gather_x(n, rows, buf, across_send, across_recv, pair_send, pair_recv):
    me = lax.axis_index("gx")
    chips = n // 2
    chip, core = me // 2, me % 2
    other = chip * 2 + 1 - core

    def block(device):
        return buf.at[pl.ds(pl.multiple_of(device * rows, ROWS), rows)]

    across, pair = [], []
    for d in range(1, chips):
        target = ((chip + d) % chips) * 2 + core
        copy = remote(block(me), block(me), across_send.at[d], across_recv.at[d], gx=target)
        copy.start()
        across.append(copy)
    copy = remote(block(me), block(me), pair_send.at[0], pair_recv.at[0], gx=other)
    copy.start()
    pair.append(copy)
    for d in range(1, chips):
        source = ((chip - d + chips) % chips) * 2 + core
        across[d - 1].wait_recv()
        copy = remote(block(source), block(source), pair_send.at[d], pair_recv.at[d], gx=other)
        copy.start()
        pair.append(copy)
    for copy in pair:
        copy.wait_recv()
    return across + pair


def gather_y(p, width, src, buf, send, recv):
    me = lax.axis_index("gy")
    columns = pl.ds(pl.multiple_of(me * width, width), width)
    copies = []
    for d in range(1, p):
        copy = remote(src, buf.at[:, columns], send.at[d], recv.at[d], gy=(me + d) % p)
        copy.start()
        copies.append(copy)
    buf[:, columns] = src[...]
    for copy in copies:
        copy.wait_recv()
    return copies


def kernel(
    n, p, u_ref, v_ref, sea_ref, bottom_ref, project_ref, fx_ref, fy_ref, ix_ref, iy_ref, ex_ref, ey_ref,
    shape_ref, shift_ref, uc_ref, vc_ref, p_ref,
    weights, fu, fv, xsend, xrecv, ysend, yrecv, xg, xg2, ysrc, ysrc2, yg, yg2, ixe, pp, grad, psend, precv, denom,
    edge_s, edge_r, ye_s, ye_r, pe_s, pe_r, as1, ar1, ps1, pr1, as2, ar2, ps2, pr2, ys1, yr1, ys2, yr2,
):
    levels, rows, width = u_ref.shape
    me_x, me_y = lax.axis_index("gx"), lax.axis_index("gy")
    left, right = (me_x + n - 1) % n, (me_x + 1) % n
    barrier = pltpu.get_barrier_semaphore()
    for d in range(1, n):
        pl.semaphore_signal(barrier, inc=1, device_id={"gx": (me_x + d) % n}, device_id_type=MESH)
    for d in range(1, p):
        pl.semaphore_signal(barrier, inc=1, device_id={"gy": (me_y + d) % p}, device_id_type=MESH)

    table = project_ref[...].astype(F32)
    for level in range(levels):
        for mode in range(2):
            weights[2 * level + mode] = jnp.broadcast_to(
                table[level : level + 1, mode : mode + 1], (ROWS, width)
            )

    def depth_of(at):
        return jnp.where(sea_ref[at, :] > 0, bottom_ref[at, :], 0)

    def project(ref, out, pad, step):
        at = pl.ds(pl.multiple_of(step * ROWS, ROWS), ROWS)
        depth = depth_of(at)
        sums = [jnp.zeros((ROWS, width), F32)] * 2
        for level in range(levels):
            value = jnp.where(level < depth, ref[level, at, :].astype(F32), 0.0)
            for mode in range(2):
                sums[mode] = sums[mode] + weights[2 * level + mode] * value
        to = pl.ds(pl.multiple_of(step * ROWS + pad, 8), ROWS)
        for mode in range(2):
            out[mode, to, :] = sums[mode].astype(BF16).astype(F32)

    def edges(first, second, out):
        lane = lax.broadcasted_iota(jnp.int32, (rows, width), 1)
        out[0] = jnp.where(lane == 0, first, pltpu.roll(second, 1, 1)).astype(BF16)
        out[1] = jnp.where(lane == width - 1, first, pltpu.roll(second, width - 1, 1)).astype(BF16)

    def swap_y(src, dst, send, recv, act):
        down = remote(src.at[0], dst.at[1], send.at[0], recv.at[1], gy=jnp.maximum(me_y - 1, 0))
        up = remote(src.at[1], dst.at[0], send.at[1], recv.at[0], gy=jnp.minimum(me_y + 1, p - 1))

        @pl.when(me_y > 0)
        def _():
            if act == "start":
                down.start()
            if act == "send":
                down.wait_send()
            if act == "recv":
                up.wait_recv()

        @pl.when(me_y < p - 1)
        def _():
            if act == "start":
                up.start()
            if act == "send":
                up.wait_send()
            if act == "recv":
                down.wait_recv()

    def difference_y(field, halo, mode):
        lane = lax.broadcasted_iota(jnp.int32, (rows, width), 1)
        low, high = halo[0].astype(F32), halo[1].astype(F32)
        before = jnp.where(lane == 0, pltpu.roll(low, 1 + mode, 1), pltpu.roll(field, 1, 1))
        after = jnp.where(
            lane == width - 1, pltpu.roll(high, width - 1 - mode, 1), pltpu.roll(field, width - 1, 1)
        )
        return 0.5 * (after - before)

    @pl.when(me_y == 0)
    def _():
        yrecv[0] = jnp.zeros((rows, width), BF16)
        precv[0] = jnp.zeros((rows, width), BF16)

    @pl.when(me_y == p - 1)
    def _():
        yrecv[1] = jnp.zeros((rows, width), BF16)
        precv[1] = jnp.zeros((rows, width), BF16)

    steps = rows // ROWS
    project(u_ref, fu, PAD, 0)
    project(u_ref, fu, PAD, steps - 1)
    xsend[...] = jnp.zeros(xsend.shape, F32)
    for mode in range(2):
        xsend[0, mode : mode + 1, :] = fu[mode, PAD : PAD + 1, :]
        xsend[1, mode : mode + 1, :] = fu[mode, PAD + rows - 1 : PAD + rows, :]

    pl.semaphore_wait(barrier, n - 1 + p - 1)
    to_left = remote(xsend.at[0], xrecv.at[1], edge_s.at[0], edge_r.at[0], gx=left)
    to_right = remote(xsend.at[1], xrecv.at[0], edge_s.at[1], edge_r.at[1], gx=right)
    to_left.start()
    to_right.start()

    def project_v(step, carry):
        project(v_ref, fv, 0, step)
        return carry

    def project_u(step, carry):
        project(u_ref, fu, PAD, step)
        return carry

    lax.fori_loop(0, steps, project_v, 0)
    edges(fv[0], fv[1], ysend)
    swap_y(ysend, yrecv, ye_s, ye_r, "start")
    lax.fori_loop(1, steps - 1, project_u, 0)

    to_left.wait_recv()
    to_right.wait_recv()
    for mode in range(2):
        fu[mode, PAD - 1 : PAD, :] = xrecv[0, mode : mode + 1, :]
        fu[mode, PAD + rows : PAD + rows + 1, :] = xrecv[1, mode : mode + 1, :]
    swap_y(ysend, yrecv, ye_s, ye_r, "recv")
    sea = sea_ref[...].astype(F32)
    mine = pl.ds(pl.multiple_of(me_x * rows, ROWS), rows)
    for mode in range(2):
        along_x = 0.5 * (
            fu[mode, PAD + 1 : PAD + 1 + rows, :] - fu[mode, PAD - 1 : PAD - 1 + rows, :]
        )
        along_y = difference_y(fv[mode], yrecv, mode)
        xg[mine, mode * width : (mode + 1) * width] = (sea * (along_x + along_y)).astype(BF16)
    sent = gather_x(n, rows, xg, as1, ar1, ps1, pr1)

    rows_left = remote(ix_ref.at[0:ROWS], ixe.at[ROWS : 2 * ROWS], edge_s.at[2], edge_r.at[2], gx=left)
    rows_right = remote(
        ix_ref.at[rows - ROWS : rows], ixe.at[0:ROWS], edge_s.at[3], edge_r.at[3], gx=right
    )
    rows_left.start()
    rows_right.start()
    spectrum = jnp.dot(fx_ref[...], xg[...], preferred_element_type=F32)
    for mode in range(2):
        ysrc[mode * rows : (mode + 1) * rows, :] = spectrum[:, mode * width : (mode + 1) * width].astype(BF16)
    row = lax.broadcasted_iota(jnp.int32, (rows, rows), 0)
    column = lax.broadcasted_iota(jnp.int32, (rows, rows), 1)
    ex = jnp.sum(jnp.where(row == column, ex_ref[...], 0.0), axis=1, keepdims=True)
    for mode in range(2):
        denom[mode * rows : (mode + 1) * rows, :] = ex + ey_ref[...] + shift_ref[mode]
    sent += gather_y(p, width, ysrc, yg, ys1, yr1)
    spectrum = lax.dot_general(yg[...], fy_ref[...], LAST, preferred_element_type=F32)
    ysrc2[...] = (spectrum / denom[...]).astype(BF16)
    sent += gather_y(p, width, ysrc2, yg2, ys2, yr2)
    back = lax.dot_general(yg2[...], iy_ref[...], LAST, preferred_element_type=F32).astype(BF16)
    for mode in range(2):
        xg2[mine, mode * width : (mode + 1) * width] = back[mode * rows : (mode + 1) * rows]
    sent += gather_x(n, rows, xg2, as2, ar2, ps2, pr2)

    pressure = jnp.dot(ix_ref[...], xg2[...], preferred_element_type=F32)
    fields = [pressure[:, mode * width : (mode + 1) * width] for mode in range(2)]
    edges(fields[0], fields[1], psend)
    swap_y(psend, precv, pe_s, pe_r, "start")
    for mode in range(2):
        p_ref[mode] = fields[mode]
        pp[mode, PAD : PAD + rows, :] = fields[mode]
    rows_left.wait_recv()
    rows_right.wait_recv()
    outside = jnp.dot(ixe[...], xg2[...], preferred_element_type=F32)
    for mode in range(2):
        part = outside[:, mode * width : (mode + 1) * width]
        pp[mode, PAD - 1 : PAD, :] = part[ROWS - 1 : ROWS]
        pp[mode, PAD + rows : PAD + rows + 1, :] = part[ROWS : ROWS + 1]
    for mode in range(2):
        grad[mode] = 0.5 * (
            pp[mode, PAD + 1 : PAD + 1 + rows, :] - pp[mode, PAD - 1 : PAD - 1 + rows, :]
        )

    def rebuild(out):
        def one(step, carry):
            at = pl.ds(pl.multiple_of(step * ROWS, ROWS), ROWS)
            depth = depth_of(at)
            zero, one = grad[0, at, :], grad[1, at, :]
            for level in range(levels):
                value = -(shape_ref[level, 0] * zero + shape_ref[level, 1] * one)
                out[level, at, :] = jnp.where(level < depth, value, 0.0).astype(BF16)
            return carry

        lax.fori_loop(0, steps, one, 0)

    rebuild(uc_ref)
    swap_y(psend, precv, pe_s, pe_r, "recv")
    for mode in range(2):
        grad[mode] = difference_y(p_ref[mode], precv, mode)
    rebuild(vc_ref)

    for copy in sent + [to_left, to_right, rows_left, rows_right]:
        copy.wait_send()
    swap_y(ysend, yrecv, ye_s, ye_r, "send")
    swap_y(psend, precv, pe_s, pe_r, "send")


def body(
    n,
    p,
    u_flow,
    v_flow,
    sea_mask,
    bottom_level,
    mode_project,
    mode_shape,
    forward_x,
    forward_y,
    inverse_x,
    inverse_y,
    eigen_x,
    eigen_y,
    mode_shift,
):
    levels, rows, width = u_flow.shape
    nx, ny = n * rows, p * width
    vmem = pl.BlockSpec(memory_space=pltpu.VMEM)
    smem = pl.BlockSpec(memory_space=pltpu.SMEM)
    dma = pltpu.SemaphoreType.DMA
    chips = n // 2
    return pl.pallas_call(
        functools.partial(kernel, n, p),
        out_shape=(
            jax.ShapeDtypeStruct(u_flow.shape, BF16),
            jax.ShapeDtypeStruct(v_flow.shape, BF16),
            jax.ShapeDtypeStruct((2, rows, width), F32),
        ),
        in_specs=[vmem] * 11 + [smem] * 2,
        out_specs=(vmem,) * 3,
        scratch_shapes=[
            pltpu.VMEM((2 * levels, ROWS, width), F32),
            pltpu.VMEM((2, rows + 2 * PAD, width), F32),
            pltpu.VMEM((2, rows, width), F32),
            pltpu.VMEM((2, 8, width), F32),
            pltpu.VMEM((2, 8, width), F32),
            pltpu.VMEM((2, rows, width), BF16),
            pltpu.VMEM((2, rows, width), BF16),
            pltpu.VMEM((nx, 2 * width), BF16),
            pltpu.VMEM((nx, 2 * width), BF16),
            pltpu.VMEM((2 * rows, width), BF16),
            pltpu.VMEM((2 * rows, width), BF16),
            pltpu.VMEM((2 * rows, ny), BF16),
            pltpu.VMEM((2 * rows, ny), BF16),
            pltpu.VMEM((2 * ROWS, nx), BF16),
            pltpu.VMEM((2, rows + 2 * PAD, width), F32),
            pltpu.VMEM((2, rows, width), F32),
            pltpu.VMEM((2, rows, width), BF16),
            pltpu.VMEM((2, rows, width), BF16),
            pltpu.VMEM((2 * rows, width), F32),
            dma((4,)),
            dma((4,)),
            dma((2,)),
            dma((2,)),
            dma((2,)),
            dma((2,)),
        ]
        + [dma((chips,))] * 8
        + [dma((p,))] * 4,
        compiler_params=pltpu.CompilerParams(
            collective_id=0, has_side_effects=True, vmem_limit_bytes=56 * 2**20
        ),
        cost_estimate=pl.CostEstimate(
            flops=8 * rows * width * (nx + ny), bytes_accessed=8 * u_flow.size, transcendentals=0
        ),
    )(
        u_flow,
        v_flow,
        sea_mask,
        bottom_level,
        mode_project,
        forward_x,
        forward_y,
        inverse_x,
        inverse_y,
        eigen_x[None],
        eigen_y[None],
        mode_shape,
        mode_shift,
    )


def solution(mesh):
    return jax.shard_map(
        functools.partial(body, mesh.shape["gx"], mesh.shape["gy"]),
        mesh=mesh,
        in_specs=(
            P(None, "gx", "gy"),
            P(None, "gx", "gy"),
            P("gx", "gy"),
            P("gx", "gy"),
            P(),
            P(),
            P("gx", None),
            P("gy", None),
            P("gx", None),
            P("gy", None),
            P("gx"),
            P("gy"),
            P(),
        ),
        out_specs=(P(None, "gx", "gy"), P(None, "gx", "gy"), P(None, "gx", "gy")),
        check_vma=False,
    )
```

time: 95.9 us -> 49.6 us (0.52)
  blocking collectives: 62.7 us -> 0 us
  Pallas kernels: 0 us -> 43 us
  starting transfers between devices: 14.1 us -> 0 us
  waiting for transfers between devices: 9.56 us -> 0 us
  other arithmetic: 5.01 us -> 0 us
  local copies, waits for them, and re-layouts: 1.19 us -> 5.68 us
  matrix products: 1.96 us -> 0 us
    all_gather x6 -> x0, blocking collectives: 62.7 us -> none  [the longest x4 35.8 us: fold_x(): lax.all_gather(data, 'gx', axis=1, tiled=True)]
    pallas_call x0 -> x1, Pallas kernels: none -> 43 us  [body(): pl.pallas_call(functools.partial(kernel, n, p), out_shape=(jax.ShapeDtype...]
    ppermute x8 -> x0, starting transfers between devices: 14.1 us -> none  [the longest x4 7.83 us: extended(): lax.ppermute(lax.slice_in_dim(block, 0, width, axis=dim), axis, backward)]
    ppermute x8 -> x0, waiting for transfers between devices: 9.56 us -> none  [the longest x4 8.61 us: extended(): lax.ppermute(lax.slice_in_dim(block, 0, width, axis=dim), axis, backward)]
    unnamed x22 -> x13, local copies, waits for them, and re-layouts: 0.79 us -> 5.68 us
    convert_element_type x7 -> x0, other arithmetic: 3.12 us -> none  [the longest x1 1.57 us: body(): (-wet_f * (shape_zero * grad_y[0][None] + shape_one * grad_y[1][None])).a...]
    dot_general x8 -> x0, matrix products: 1.96 us -> none  [the longest x4 1.04 us: fold_x(): jnp.einsum('kn,mnj->mkj', table, lax.all_gather(data, 'gx', axis=1, tiled...]
    mul x4 -> x0, other arithmetic: 1.8 us -> none  [the longest x1 1.66 us: body(): u_flow * wet]
  transfers between devices with their start and end apart: 8 -> 0, of which waited for: 4 -> 0; matrix products, arithmetic and copies ran while one was open for 1% -> 0% of each run, Pallas kernels for 0% -> 0%
where the time goes in v1:
time: 49.6 us; the launch traced here: 49.3 us
  Pallas kernels  43 us (87%)
  local copies, waits for them, and re-layouts  5.68 us (11%)
  between operations  0.66 us (1%)
    pallas_call x1, Pallas kernels, body(): pl.pallas_call(functools.partial(kernel, n, p), out_shape=(jax.ShapeDtype...  43 us
    unnamed x13, local copies, waits for them, and re-layouts  5.68 us

profile of v1, /device:TPU:0, one launch (start us, length us, event | category | flops | bytes accessed | tf_op | source)
XLA Modules:
  0.0 49.3 jit_solution(2998374118137090508)
XLA Ops:
  0.6 0.0 copy-start.3
  0.6 0.6 %copy-done.3 = bf16[16,2]{0,1:T(2,128)(2,1)S(1)} copy-done((bf16[16,2]{0,1:T(2,128)(2,1)S(1)}, bf16[16,2]{0,1:T(2,128)(2,1)}, u32[]{:S(2)}) %copy-start.3) | copy-done | bytes 88
  1.3 0.0 copy-start.2
  1.3 0.7 %copy.16.project_ref = bf16[16,2]{1,0:T(8,128)(2,1)} copy(bf16[16,2]{0,1:T(2,128)(2,1)S(1)} %copy-done.3) | data formatting | bytes 128 | tf_op args[4]
  2.0 0.0 copy-done.2
  2.0 0.7 %copy.17.shape_ref = f32[16,2]{1,0:T(8,128)} copy(f32[16,2]{0,1:T(2,128)S(1)} %copy-done.2) | data formatting | bytes 256 | tf_op args[5]
  2.7 43.0 %shard_map.148 = (bf16[16,144,128]{2,1,0:T(8,128)(2,1)}, bf16[16,144,128]{2,1,0:T(8,128)(2,1)}, f32[2,144,128]{2,1,0:T(8,128)}) custom-call(bf16[16,144,128]{2,1,0:T(8,128)(2,1)} %u_ref.1, bf16[16,144,128]{2,1,0:T(8,128)(2,1)} %v_ref.1, s32[144,128]{1,0:T(8,128)} %sea_ref.1, s32[144,128]{1,0:T(8,128)} %bottom_ref.1, bf16[16,2]{1,0:T(8,128)(2,1)} %copy.16.project_ref, ...), custom_call_target="tpu_custom_call" | custom-call | flops 245366784 | bytes 2359296 | tf_op jit(solution)/shard_map/pallas_call | solution.py:281
  45.7 0.0 copy-start
  45.7 2.0 %copy.21 = bf16[16,144,128]{2,1,0:T(8,128)(2,1)} copy(bf16[16,144,128]{2,1,0:T(8,128)(2,1)} %get-tuple-element.6) | data formatting | bytes 1179648
  47.6 0.0 copy-done
  47.6 0.0 copy-start.1
  47.7 0.8 %copy.22 = bf16[16,144,128]{2,1,0:T(8,128)(2,1)} copy(bf16[16,144,128]{2,1,0:T(8,128)(2,1)S(1)} %copy-done) | data formatting | bytes 1179648
  48.5 0.2 copy-done.1
  48.7 0.7 %copy.23 = f32[2,144,128]{2,1,0:T(8,128)} copy(f32[2,144,128]{2,1,0:T(8,128)S(1)} %copy-done.1) | data formatting | bytes 294912
Async XLA Ops:
  0.6 0.7 %copy-start.3 = (bf16[16,2]{0,1:T(2,128)(2,1)S(1)}, bf16[16,2]{0,1:T(2,128)(2,1)}, u32[]{:S(2)}) copy-start(bf16[16,2]{0,1:T(2,128)(2,1)} %param.17) | copy-start | bytes 196
  1.3 0.7 %copy-start.2 = (f32[16,2]{0,1:T(2,128)S(1)}, f32[16,2]{0,1:T(2,128)}, u32[]{:S(2)}) copy-start(f32[16,2]{0,1:T(2,128)} %param.18) | copy-start | bytes 388
  45.7 2.0 %copy-start = (bf16[16,144,128]{2,1,0:T(8,128)(2,1)S(1)}, bf16[16,144,128]{2,1,0:T(8,128)(2,1)}, u32[]{:S(2)}) copy-start(bf16[16,144,128]{2,1,0:T(8,128)(2,1)} %get-tuple-element.7) | copy-start | bytes 1769476
  47.6 1.0 %copy-start.1 = (f32[2,144,128]{2,1,0:T(8,128)S(1)}, f32[2,144,128]{2,1,0:T(8,128)}, u32[]{:S(2)}) copy-start(f32[2,144,128]{2,1,0:T(8,128)} %get-tuple-element.8) | copy-start | bytes 442372

commit v2 on v1

v2 whole, which is shorter than its diff:
```python
import functools

import jax
import jax.numpy as jnp
from jax import lax
from jax.experimental import pallas as pl
from jax.experimental.pallas import tpu as pltpu
from jax.sharding import PartitionSpec as P

F32, BF16 = jnp.float32, jnp.bfloat16
ROWS = 16
PAD = 8
MESH = pl.DeviceIdType.MESH
LAST = (((1,), (1,)), ((), ()))


def remote(src, dst, send, recv, **device):
    return pltpu.make_async_remote_copy(
        src_ref=src, dst_ref=dst, send_sem=send, recv_sem=recv, device_id=device, device_id_type=MESH
    )


class AcrossX:
    def __init__(self, n, rows, buf, across_send, across_recv, pair_send, pair_recv):
        me = lax.axis_index("gx")
        chips = n // 2
        chip, core = me // 2, me % 2
        other = chip * 2 + 1 - core

        def block(device):
            return buf.at[pl.ds(pl.multiple_of(device * rows, ROWS), rows)]

        self.across, self.pair = [], []
        for d in range(chips):
            source = ((chip - d + chips) % chips) * 2 + core
            target = ((chip + d) % chips) * 2 + core
            self.pair.append(remote(block(source), block(source), pair_send.at[d], pair_recv.at[d], gx=other))
            if d > 0:
                self.across.append(
                    remote(block(me), block(me), across_send.at[d], across_recv.at[d], gx=target)
                )

    def start(self):
        for copy in self.across:
            copy.start()
        self.pair[0].start()

    def finish(self):
        for arrival, onward in zip(self.across, self.pair[1:]):
            arrival.wait_recv()
            onward.start()
        for copy in self.pair:
            copy.wait_recv()

    def wait_send(self):
        for copy in self.across + self.pair:
            copy.wait_send()


class AcrossY:
    def __init__(self, p, width, src, buf, send, recv):
        me = lax.axis_index("gy")
        columns = pl.ds(pl.multiple_of(me * width, width), width)
        self.own = (src, buf, columns)
        self.copies = [
            remote(src, buf.at[:, columns], send.at[d], recv.at[d], gy=(me + d) % p) for d in range(1, p)
        ]

    def start(self):
        src, buf, columns = self.own
        for copy in self.copies:
            copy.start()
        buf[:, columns] = src[...]

    def finish(self):
        for copy in self.copies:
            copy.wait_recv()

    def wait_send(self):
        for copy in self.copies:
            copy.wait_send()


def depth_of(sea_ref, bottom_ref, at):
    return jnp.where(sea_ref[at, :] > 0, bottom_ref[at, :], 0)


def rebuild_kernel(gx_ref, gy_ref, pressure_ref, sea_ref, bottom_ref, shape_ref, uc_ref, vc_ref, p_ref):
    levels, rows, _ = uc_ref.shape
    p_ref[...] = pressure_ref[...]

    def one(step, carry):
        at = pl.ds(pl.multiple_of(step * ROWS, ROWS), ROWS)
        depth = depth_of(sea_ref, bottom_ref, at)
        for grad, out in ((gx_ref, uc_ref), (gy_ref, vc_ref)):
            first, second = grad[0, at, :], grad[1, at, :]
            for level in range(levels):
                value = -(shape_ref[0, level] * first + shape_ref[1, level] * second)
                out[level, at, :] = jnp.where(level < depth, value, 0.0).astype(BF16)
        return carry

    lax.fori_loop(0, rows // ROWS, one, 0)


def kernel(
    n, p, u_hbm, v_hbm, sea_hbm, bottom_hbm, fx_hbm, fy_hbm, ix_hbm, iy_hbm, project_ref, ex_ref, ey_ref,
    shift_ref, gx_ref, gy_ref, p_ref,
    u_ref, v_ref, sea_ref, bottom_ref, fx_ref, fy_ref, ix_ref, iy_ref, loaded,
    weights, fu, fv, xsend, xrecv, ysend, yrecv, xg, xg2, ysrc, ysrc2, yg, yg2, ixe, pp, psend, precv, denom,
    edge_s, edge_r, ye_s, ye_r, pe_s, pe_r, as1, ar1, ps1, pr1, as2, ar2, ps2, pr2, ys1, yr1, ys2, yr2,
):
    levels, rows, width = u_ref.shape
    pairs = (
        (sea_hbm, sea_ref),
        (bottom_hbm, bottom_ref),
        (u_hbm, u_ref),
        (v_hbm, v_ref),
        (ix_hbm, ix_ref),
        (fx_hbm, fx_ref),
        (fy_hbm, fy_ref),
        (iy_hbm, iy_ref),
    )
    loads = [pltpu.make_async_copy(src, dst, loaded.at[i]) for i, (src, dst) in enumerate(pairs)]
    for load in loads:
        load.start()
    me_x, me_y = lax.axis_index("gx"), lax.axis_index("gy")
    left, right = (me_x + n - 1) % n, (me_x + 1) % n
    barrier = pltpu.get_barrier_semaphore()
    for d in range(1, n):
        pl.semaphore_signal(barrier, inc=1, device_id={"gx": (me_x + d) % n}, device_id_type=MESH)
    for d in range(1, p):
        pl.semaphore_signal(barrier, inc=1, device_id={"gy": (me_y + d) % p}, device_id_type=MESH)

    table = project_ref[...].astype(F32)
    for level in range(levels):
        for mode in range(2):
            weights[2 * level + mode] = jnp.broadcast_to(
                table[mode : mode + 1, level : level + 1], (ROWS, width)
            )

    def project(ref, out, pad, step):
        at = pl.ds(pl.multiple_of(step * ROWS, ROWS), ROWS)
        depth = depth_of(sea_ref, bottom_ref, at)
        sums = [jnp.zeros((ROWS, width), F32)] * 2
        for level in range(levels):
            value = jnp.where(level < depth, ref[level, at, :].astype(F32), 0.0)
            for mode in range(2):
                sums[mode] = sums[mode] + weights[2 * level + mode] * value
        to = pl.ds(pl.multiple_of(step * ROWS + pad, 8), ROWS)
        for mode in range(2):
            out[mode, to, :] = sums[mode].astype(BF16).astype(F32)

    def edges(first, second, out):
        lane = lax.broadcasted_iota(jnp.int32, (rows, width), 1)
        out[0] = jnp.where(lane == 0, first, pltpu.roll(second, 1, 1)).astype(BF16)
        out[1] = jnp.where(lane == width - 1, first, pltpu.roll(second, width - 1, 1)).astype(BF16)

    def swap_y(src, dst, send, recv, act):
        down = remote(src.at[0], dst.at[1], send.at[0], recv.at[1], gy=jnp.maximum(me_y - 1, 0))
        up = remote(src.at[1], dst.at[0], send.at[1], recv.at[0], gy=jnp.minimum(me_y + 1, p - 1))

        @pl.when(me_y > 0)
        def _():
            if act == "start":
                down.start()
            if act == "send":
                down.wait_send()
            if act == "recv":
                up.wait_recv()

        @pl.when(me_y < p - 1)
        def _():
            if act == "start":
                up.start()
            if act == "send":
                up.wait_send()
            if act == "recv":
                down.wait_recv()

    def difference_y(field, halo, mode):
        lane = lax.broadcasted_iota(jnp.int32, (rows, width), 1)
        low, high = halo[0].astype(F32), halo[1].astype(F32)
        before = jnp.where(lane == 0, pltpu.roll(low, 1 + mode, 1), pltpu.roll(field, 1, 1))
        after = jnp.where(
            lane == width - 1, pltpu.roll(high, width - 1 - mode, 1), pltpu.roll(field, width - 1, 1)
        )
        return 0.5 * (after - before)

    @pl.when(me_y == 0)
    def _():
        yrecv[0] = jnp.zeros((rows, width), BF16)
        precv[0] = jnp.zeros((rows, width), BF16)

    @pl.when(me_y == p - 1)
    def _():
        yrecv[1] = jnp.zeros((rows, width), BF16)
        precv[1] = jnp.zeros((rows, width), BF16)

    steps = rows // ROWS
    for load in loads[:3]:
        load.wait()
    project(u_ref, fu, PAD, 0)
    project(u_ref, fu, PAD, steps - 1)
    xsend[...] = jnp.zeros(xsend.shape, F32)
    for mode in range(2):
        xsend[0, mode : mode + 1, :] = fu[mode, PAD : PAD + 1, :]
        xsend[1, mode : mode + 1, :] = fu[mode, PAD + rows - 1 : PAD + rows, :]

    pl.semaphore_wait(barrier, n - 1 + p - 1)
    to_left = remote(xsend.at[0], xrecv.at[1], edge_s.at[0], edge_r.at[0], gx=left)
    to_right = remote(xsend.at[1], xrecv.at[0], edge_s.at[1], edge_r.at[1], gx=right)
    to_left.start()
    to_right.start()

    def project_v(step, carry):
        project(v_ref, fv, 0, step)
        return carry

    def project_u(step, carry):
        project(u_ref, fu, PAD, step)
        return carry

    loads[3].wait()
    lax.fori_loop(0, steps, project_v, 0)
    edges(fv[0], fv[1], ysend)
    swap_y(ysend, yrecv, ye_s, ye_r, "start")
    lax.fori_loop(1, steps - 1, project_u, 0)

    to_left.wait_recv()
    to_right.wait_recv()
    for mode in range(2):
        fu[mode, PAD - 1 : PAD, :] = xrecv[0, mode : mode + 1, :]
        fu[mode, PAD + rows : PAD + rows + 1, :] = xrecv[1, mode : mode + 1, :]
    swap_y(ysend, yrecv, ye_s, ye_r, "recv")
    sea = sea_ref[...].astype(F32)
    mine = pl.ds(pl.multiple_of(me_x * rows, ROWS), rows)
    modes = range(2)
    gx1 = [AcrossX(n, rows, xg.at[m], as1.at[m], ar1.at[m], ps1.at[m], pr1.at[m]) for m in modes]
    gx2 = [AcrossX(n, rows, xg2.at[m], as2.at[m], ar2.at[m], ps2.at[m], pr2.at[m]) for m in modes]
    gy1 = [AcrossY(p, width, ysrc.at[m], yg.at[m], ys1.at[m], yr1.at[m]) for m in modes]
    gy2 = [AcrossY(p, width, ysrc2.at[m], yg2.at[m], ys2.at[m], yr2.at[m]) for m in modes]
    for mode in modes:
        along_x = 0.5 * (
            fu[mode, PAD + 1 : PAD + 1 + rows, :] - fu[mode, PAD - 1 : PAD - 1 + rows, :]
        )
        along_y = difference_y(fv[mode], yrecv, mode)
        xg[mode, mine, :] = (sea * (along_x + along_y)).astype(BF16)
        gx1[mode].start()

    for load in loads[4:]:
        load.wait()
    rows_left = remote(ix_ref.at[0:ROWS], ixe.at[ROWS : 2 * ROWS], edge_s.at[2], edge_r.at[2], gx=left)
    rows_right = remote(
        ix_ref.at[rows - ROWS : rows], ixe.at[0:ROWS], edge_s.at[3], edge_r.at[3], gx=right
    )
    rows_left.start()
    rows_right.start()
    row = lax.broadcasted_iota(jnp.int32, (rows, rows), 0)
    column = lax.broadcasted_iota(jnp.int32, (rows, rows), 1)
    ex = jnp.sum(jnp.where(row == column, ex_ref[...], 0.0), axis=1, keepdims=True)
    for mode in modes:
        denom[mode] = ex + ey_ref[...] + shift_ref[mode]
    for mode in modes:
        gx1[mode].finish()
        ysrc[mode] = jnp.dot(fx_ref[...], xg[mode], preferred_element_type=F32).astype(BF16)
        gy1[mode].start()
    for mode in modes:
        gy1[mode].finish()
        spectrum = lax.dot_general(yg[mode], fy_ref[...], LAST, preferred_element_type=F32)
        ysrc2[mode] = (spectrum / denom[mode]).astype(BF16)
        gy2[mode].start()
    for mode in modes:
        gy2[mode].finish()
        back = lax.dot_general(yg2[mode], iy_ref[...], LAST, preferred_element_type=F32)
        xg2[mode, mine, :] = back.astype(BF16)
        gx2[mode].start()
    rows_left.wait_recv()
    rows_right.wait_recv()
    for mode in modes:
        gx2[mode].finish()
        field = jnp.dot(ix_ref[...], xg2[mode], preferred_element_type=F32)
        p_ref[mode] = field
        pp[mode, PAD : PAD + rows, :] = field
    edges(p_ref[0], p_ref[1], psend)
    swap_y(psend, precv, pe_s, pe_r, "start")
    for mode in modes:
        outside = jnp.dot(ixe[...], xg2[mode], preferred_element_type=F32)
        pp[mode, PAD - 1 : PAD, :] = outside[ROWS - 1 : ROWS]
        pp[mode, PAD + rows : PAD + rows + 1, :] = outside[ROWS : ROWS + 1]
        gx_ref[mode] = 0.5 * (
            pp[mode, PAD + 1 : PAD + 1 + rows, :] - pp[mode, PAD - 1 : PAD - 1 + rows, :]
        )
    for copy in gx1 + gx2 + gy1 + gy2 + [to_left, to_right, rows_left, rows_right]:
        copy.wait_send()
    swap_y(ysend, yrecv, ye_s, ye_r, "send")
    swap_y(psend, precv, pe_s, pe_r, "recv")
    for mode in modes:
        gy_ref[mode] = difference_y(p_ref[mode], precv, mode)
    swap_y(psend, precv, pe_s, pe_r, "send")


def body(
    n,
    p,
    u_flow,
    v_flow,
    sea_mask,
    bottom_level,
    mode_project,
    mode_shape,
    forward_x,
    forward_y,
    inverse_x,
    inverse_y,
    eigen_x,
    eigen_y,
    mode_shift,
):
    levels, rows, width = u_flow.shape
    nx, ny = n * rows, p * width
    vmem = pl.BlockSpec(memory_space=pltpu.VMEM)
    smem = pl.BlockSpec(memory_space=pltpu.SMEM)
    dma = pltpu.SemaphoreType.DMA
    chips = n // 2
    field = jax.ShapeDtypeStruct((2, rows, width), F32)
    grad_x, grad_y, pressure = pl.pallas_call(
        functools.partial(kernel, n, p),
        out_shape=(field,) * 3,
        in_specs=[pl.BlockSpec(memory_space=pl.ANY)] * 8 + [vmem] * 3 + [smem],
        out_specs=(vmem,) * 3,
        scratch_shapes=[
            pltpu.VMEM(source.shape, source.dtype)
            for source in (
                u_flow, v_flow, sea_mask, bottom_level, forward_x, forward_y, inverse_x, inverse_y
            )
        ]
        + [dma((8,))]
        + [
            pltpu.VMEM((2 * levels, ROWS, width), F32),
            pltpu.VMEM((2, rows + 2 * PAD, width), F32),
            pltpu.VMEM((2, rows, width), F32),
            pltpu.VMEM((2, 8, width), F32),
            pltpu.VMEM((2, 8, width), F32),
            pltpu.VMEM((2, rows, width), BF16),
            pltpu.VMEM((2, rows, width), BF16),
            pltpu.VMEM((2, nx, width), BF16),
            pltpu.VMEM((2, nx, width), BF16),
            pltpu.VMEM((2, rows, width), BF16),
            pltpu.VMEM((2, rows, width), BF16),
            pltpu.VMEM((2, rows, ny), BF16),
            pltpu.VMEM((2, rows, ny), BF16),
            pltpu.VMEM((2 * ROWS, nx), BF16),
            pltpu.VMEM((2, rows + 2 * PAD, width), F32),
            pltpu.VMEM((2, rows, width), BF16),
            pltpu.VMEM((2, rows, width), BF16),
            pltpu.VMEM((2, rows, width), F32),
            dma((4,)),
            dma((4,)),
            dma((2,)),
            dma((2,)),
            dma((2,)),
            dma((2,)),
        ]
        + [dma((2, chips))] * 8
        + [dma((2, p))] * 4,
        compiler_params=pltpu.CompilerParams(
            collective_id=0, has_side_effects=True, vmem_limit_bytes=56 * 2**20
        ),
        cost_estimate=pl.CostEstimate(
            flops=8 * rows * width * (nx + ny), bytes_accessed=8 * u_flow.size, transcendentals=0
        ),
    )(
        u_flow,
        v_flow,
        sea_mask,
        bottom_level,
        forward_x,
        forward_y,
        inverse_x,
        inverse_y,
        mode_project.T,
        eigen_x[None],
        eigen_y[None],
        mode_shift,
    )
    return pl.pallas_call(
        rebuild_kernel,
        out_shape=(
            jax.ShapeDtypeStruct(u_flow.shape, BF16),
            jax.ShapeDtypeStruct(v_flow.shape, BF16),
            field,
        ),
        in_specs=[vmem] * 5 + [smem],
        out_specs=(vmem,) * 3,
        compiler_params=pltpu.CompilerParams(vmem_limit_bytes=56 * 2**20),
        cost_estimate=pl.CostEstimate(
            flops=8 * u_flow.size, bytes_accessed=4 * u_flow.size, transcendentals=0
        ),
    )(grad_x, grad_y, pressure, sea_mask, bottom_level, mode_shape.T)


def solution(mesh):
    return jax.shard_map(
        functools.partial(body, mesh.shape["gx"], mesh.shape["gy"]),
        mesh=mesh,
        in_specs=(
            P(None, "gx", "gy"),
            P(None, "gx", "gy"),
            P("gx", "gy"),
            P("gx", "gy"),
            P(),
            P(),
            P("gx", None),
            P("gy", None),
            P("gx", None),
            P("gy", None),
            P("gx"),
            P("gy"),
            P(),
        ),
        out_specs=(P(None, "gx", "gy"), P(None, "gx", "gy"), P(None, "gx", "gy")),
        check_vma=False,
    )
```

time: 49.6 us -> 43.5 us (0.88)
  local copies, waits for them, and re-layouts: 5.68 us -> 0 us
    unnamed x13 -> x0, local copies, waits for them, and re-layouts: 5.68 us -> none
    pallas_call x1 -> x2, Pallas kernels: 43 us -> 42.7 us  [the longest x1 39.9 us: body(): pl.pallas_call(functools.partial(kernel, n, p), out_shape=(field,) * 3, i...]
where the time goes in v2:
time: 43.5 us; the launch traced here: 43.3 us
  Pallas kernels  42.7 us (98%)
  between operations  0.64 us (1%)
    pallas_call x1, Pallas kernels, body(): pl.pallas_call(functools.partial(kernel, n, p), out_shape=(field,) * 3, i...  39.9 us
    pallas_call x1, Pallas kernels, body(): pl.pallas_call(rebuild_kernel, out_shape=(jax.ShapeDtypeStruct(u_flow.sha...  2.75 us

profile of v2, /device:TPU:0, one launch (start us, length us, event | category | flops | bytes accessed | tf_op | source)
XLA Modules:
  0.0 43.3 jit_solution(5318132790329581570)
XLA Ops:
  0.6 39.9 %shard_map.148 = (f32[2,144,128]{2,1,0:T(8,128)}, f32[2,144,128]{2,1,0:T(8,128)}, f32[2,144,128]{2,1,0:T(8,128)}) custom-call(bf16[16,144,128]{2,1,0:T(8,128)(2,1)} %u_hbm.1, bf16[16,144,128]{2,1,0:T(8,128)(2,1)} %v_hbm.1, s32[144,128]{1,0:T(8,128)} %sea_ref.1, s32[144,128]{1,0:T(8,128)} %bottom_ref.1, bf16[144,1152]{1,0:T(8,128)(2,1)} %fx_hbm.1, ...), custom_call_target="tpu_custom_call" | custom-call | flops 245366784 | bytes 2359296 | tf_op jit(solution)/shard_map/pallas_call | solution.py:326
  40.6 2.7 %shard_map.149 = (bf16[16,144,128]{2,1,0:T(8,128)(2,1)}, bf16[16,144,128]{2,1,0:T(8,128)(2,1)}, f32[2,144,128]{2,1,0:T(8,128)}) custom-call(f32[2,144,128]{2,1,0:T(8,128)} %get-tuple-element.6.gx_ref, f32[2,144,128]{2,1,0:T(8,128)} %get-tuple-element.7.gy_ref, f32[2,144,128]{2,1,0:T(8,128)} %get-tuple-element.8.pressure_ref, s32[144,128]{1,0:T(8,128)} %sea_ref.1, ...), custom_call_target="tpu_custom_call" | custom-call | flops 2359296 | bytes 1179648 | tf_op jit(solution)/shard_map/pallas_call | solution.py:386

commit v3 on v2

--- a/solution.py
+++ b/solution.py
@@ -58,19 +58,18 @@
 
 
 class AcrossY:
-    def __init__(self, p, width, src, buf, send, recv):
+    def __init__(self, p, src, buf, send, recv):
         me = lax.axis_index("gy")
-        columns = pl.ds(pl.multiple_of(me * width, width), width)
-        self.own = (src, buf, columns)
+        self.own = (src, buf, me)
         self.copies = [
-            remote(src, buf.at[:, columns], send.at[d], recv.at[d], gy=(me + d) % p) for d in range(1, p)
+            remote(src, buf.at[me], send.at[d], recv.at[d], gy=(me + d) % p) for d in range(1, p)
         ]
 
     def start(self):
-        src, buf, columns = self.own
+        src, buf, me = self.own
         for copy in self.copies:
             copy.start()
-        buf[:, columns] = src[...]
+        buf[me] = src[...]
 
     def finish(self):
         for copy in self.copies:
@@ -206,23 +205,24 @@
         xsend[0, mode : mode + 1, :] = fu[mode, PAD : PAD + 1, :]
         xsend[1, mode : mode + 1, :] = fu[mode, PAD + rows - 1 : PAD + rows, :]
 
+    def project_v(step, carry):
+        project(v_ref, fv, 0, step)
+        return carry
+
+    loads[3].wait()
+    lax.fori_loop(0, steps, project_v, 0)
+    edges(fv[0], fv[1], ysend)
+
     pl.semaphore_wait(barrier, n - 1 + p - 1)
     to_left = remote(xsend.at[0], xrecv.at[1], edge_s.at[0], edge_r.at[0], gx=left)
     to_right = remote(xsend.at[1], xrecv.at[0], edge_s.at[1], edge_r.at[1], gx=right)
     to_left.start()
     to_right.start()
 
-    def project_v(step, carry):
-        project(v_ref, fv, 0, step)
-        return carry
-
     def project_u(step, carry):
         project(u_ref, fu, PAD, step)
         return carry
 
-    loads[3].wait()
-    lax.fori_loop(0, steps, project_v, 0)
-    edges(fv[0], fv[1], ysend)
     swap_y(ysend, yrecv, ye_s, ye_r, "start")
     lax.fori_loop(1, steps - 1, project_u, 0)
 
@@ -237,8 +237,8 @@
     modes = range(2)
     gx1 = [AcrossX(n, rows, xg.at[m], as1.at[m], ar1.at[m], ps1.at[m], pr1.at[m]) for m in modes]
     gx2 = [AcrossX(n, rows, xg2.at[m], as2.at[m], ar2.at[m], ps2.at[m], pr2.at[m]) for m in modes]
-    gy1 = [AcrossY(p, width, ysrc.at[m], yg.at[m], ys1.at[m], yr1.at[m]) for m in modes]
-    gy2 = [AcrossY(p, width, ysrc2.at[m], yg2.at[m], ys2.at[m], yr2.at[m]) for m in modes]
+    gy1 = [AcrossY(p, ysrc.at[m], yg.at[m], ys1.at[m], yr1.at[m]) for m in modes]
+    gy2 = [AcrossY(p, ysrc2.at[m], yg2.at[m], ys2.at[m], yr2.at[m]) for m in modes]
     for mode in modes:
         along_x = 0.5 * (
             fu[mode, PAD + 1 : PAD + 1 + rows, :] - fu[mode, PAD - 1 : PAD - 1 + rows, :]
@@ -264,14 +264,18 @@
         gx1[mode].finish()
         ysrc[mode] = jnp.dot(fx_ref[...], xg[mode], preferred_element_type=F32).astype(BF16)
         gy1[mode].start()
+
+    def whole(blocks, mode):
+        return jnp.concatenate([blocks[mode, source] for source in range(p)], axis=1)
+
     for mode in modes:
         gy1[mode].finish()
-        spectrum = lax.dot_general(yg[mode], fy_ref[...], LAST, preferred_element_type=F32)
+        spectrum = lax.dot_general(whole(yg, mode), fy_ref[...], LAST, preferred_element_type=F32)
         ysrc2[mode] = (spectrum / denom[mode]).astype(BF16)
         gy2[mode].start()
     for mode in modes:
         gy2[mode].finish()
-        back = lax.dot_general(yg2[mode], iy_ref[...], LAST, preferred_element_type=F32)
+        back = lax.dot_general(whole(yg2, mode), iy_ref[...], LAST, preferred_element_type=F32)
         xg2[mode, mine, :] = back.astype(BF16)
         gx2[mode].start()
     rows_left.wait_recv()
@@ -347,8 +351,8 @@
             pltpu.VMEM((2, nx, width), BF16),
             pltpu.VMEM((2, rows, width), BF16),
             pltpu.VMEM((2, rows, width), BF16),
-            pltpu.VMEM((2, rows, ny), BF16),
-            pltpu.VMEM((2, rows, ny), BF16),
+            pltpu.VMEM((2, p, rows, width), BF16),
+            pltpu.VMEM((2, p, rows, width), BF16),
             pltpu.VMEM((2 * ROWS, nx), BF16),
             pltpu.VMEM((2, rows + 2 * PAD, width), F32),
             pltpu.VMEM((2, rows, width), BF16),

time: 43.5 us -> 43.4 us (level)
  no operation moved by 1% of the time
where the time goes in v3:
time: 43.4 us; the launch traced here: 43.3 us
  Pallas kernels  42.6 us (98%)
  between operations  0.64 us (1%)
    pallas_call x1, Pallas kernels, body(): pl.pallas_call(functools.partial(kernel, n, p), out_shape=(field,) * 3, i...  39.9 us
    pallas_call x1, Pallas kernels, body(): pl.pallas_call(rebuild_kernel, out_shape=(jax.ShapeDtypeStruct(u_flow.sha...  2.75 us

profile of v3, /device:TPU:0, one launch (start us, length us, event | category | flops | bytes accessed | tf_op | source)
XLA Modules:
  0.0 43.3 jit_solution(15053366197260208426)
XLA Ops:
  0.6 39.9 %shard_map.148 = (f32[2,144,128]{2,1,0:T(8,128)}, f32[2,144,128]{2,1,0:T(8,128)}, f32[2,144,128]{2,1,0:T(8,128)}) custom-call(bf16[16,144,128]{2,1,0:T(8,128)(2,1)} %u_hbm.1, bf16[16,144,128]{2,1,0:T(8,128)(2,1)} %v_hbm.1, s32[144,128]{1,0:T(8,128)} %sea_ref.1, s32[144,128]{1,0:T(8,128)} %bottom_ref.1, bf16[144,1152]{1,0:T(8,128)(2,1)} %fx_hbm.1, ...), custom_call_target="tpu_custom_call" | custom-call | flops 245366784 | bytes 2359296 | tf_op jit(solution)/shard_map/pallas_call | solution.py:330
  40.5 2.7 %shard_map.149 = (bf16[16,144,128]{2,1,0:T(8,128)(2,1)}, bf16[16,144,128]{2,1,0:T(8,128)(2,1)}, f32[2,144,128]{2,1,0:T(8,128)}) custom-call(f32[2,144,128]{2,1,0:T(8,128)} %get-tuple-element.6.gx_ref, f32[2,144,128]{2,1,0:T(8,128)} %get-tuple-element.7.gy_ref, f32[2,144,128]{2,1,0:T(8,128)} %get-tuple-element.8.pressure_ref, s32[144,128]{1,0:T(8,128)} %sea_ref.1, ...), custom_call_target="tpu_custom_call" | custom-call | flops 2359296 | bytes 1179648 | tf_op jit(solution)/shard_map/pallas_call | solution.py:390

commit v4 on v3

--- a/solution.py
+++ b/solution.py
@@ -387,6 +387,10 @@
         eigen_y[None],
         mode_shift,
     )
+    part = rows // 3 if rows % (3 * ROWS) == 0 else rows
+    flat = pl.BlockSpec((part, width), lambda i: (i, 0))
+    modal = pl.BlockSpec((2, part, width), lambda i: (0, i, 0))
+    tall = pl.BlockSpec((levels, part, width), lambda i: (0, i, 0))
     return pl.pallas_call(
         rebuild_kernel,
         out_shape=(
@@ -394,8 +398,9 @@
             jax.ShapeDtypeStruct(v_flow.shape, BF16),
             field,
         ),
-        in_specs=[vmem] * 5 + [smem],
-        out_specs=(vmem,) * 3,
+        grid=(rows // part,),
+        in_specs=[modal] * 3 + [flat] * 2 + [smem],
+        out_specs=(tall, tall, modal),
         compiler_params=pltpu.CompilerParams(vmem_limit_bytes=56 * 2**20),
         cost_estimate=pl.CostEstimate(
             flops=8 * u_flow.size, bytes_accessed=4 * u_flow.size, transcendentals=0

time: 43.4 us -> 43.9 us (1.012)
  no operation moved by 1% of the time
where the time goes in v4:
time: 43.9 us; the launch traced here: 43.6 us
  Pallas kernels  42.9 us (98%)
  between operations  0.64 us (1%)
    pallas_call x1, Pallas kernels, body(): pl.pallas_call(functools.partial(kernel, n, p), out_shape=(field,) * 3, i...  39.9 us
    pallas_call x1, Pallas kernels, body(): pl.pallas_call(rebuild_kernel, out_shape=(jax.ShapeDtypeStruct(u_flow.sha...  3.07 us

profile of v4, /device:TPU:0, one launch (start us, length us, event | category | flops | bytes accessed | tf_op | source)
XLA Modules:
  0.0 43.6 jit_solution(14177780764263909830)
XLA Ops:
  0.6 39.9 %shard_map.148 = (f32[2,144,128]{2,1,0:T(8,128)}, f32[2,144,128]{2,1,0:T(8,128)}, f32[2,144,128]{2,1,0:T(8,128)}) custom-call(bf16[16,144,128]{2,1,0:T(8,128)(2,1)} %u_hbm.1, bf16[16,144,128]{2,1,0:T(8,128)(2,1)} %v_hbm.1, s32[144,128]{1,0:T(8,128)} %sea_ref.1, s32[144,128]{1,0:T(8,128)} %bottom_ref.1, bf16[144,1152]{1,0:T(8,128)(2,1)} %fx_hbm.1, ...), custom_call_target="tpu_custom_call" | custom-call | flops 245366784 | bytes 2359296 | tf_op jit(solution)/shard_map/pallas_call | solution.py:330
  40.5 3.1 %shard_map.149 = (bf16[16,144,128]{2,1,0:T(8,128)(2,1)}, bf16[16,144,128]{2,1,0:T(8,128)(2,1)}, f32[2,144,128]{2,1,0:T(8,128)}) custom-call(f32[2,144,128]{2,1,0:T(8,128)} %get-tuple-element.6.gx_ref, f32[2,144,128]{2,1,0:T(8,128)} %get-tuple-element.7.gy_ref, f32[2,144,128]{2,1,0:T(8,128)} %get-tuple-element.8.pressure_ref, s32[144,128]{1,0:T(8,128)} %sea_ref.1, ...), custom_call_target="tpu_custom_call" | custom-call | flops 2359296 | bytes 1179648 | tf_op jit(solution)/shard_map/pallas_call | solution.py:394
